TPU v7x, 32 devices: a whole 2x2x4 slice. The times are simulated.
32 devices in a mesh: groups: 2 (over y), seq: 4 (over z), head: 2 (over x), batch: 2 (over core).
Axes of the slice: x: 2, y: 2, z: 4, core: 2. Of those that a mesh axis runs over, the one named last changes fastest.
Arguments:
- queries: bfloat16 [4, 2048, 256], P(('groups', 'batch'), 'seq', 'head'), parts along dimension 0, may hold values from -8 to 8
- key_vectors: bfloat16 [4, 2048, 256], P(('groups', 'batch'), 'seq', 'head'), parts along dimension 0, may hold values from -8 to 8
- value_vectors: bfloat16 [4, 2048, 2048], P(('groups', 'batch'), 'seq', 'head'), parts along dimension 0, may hold values from -6 to 6
Outputs:
- mixture: bfloat16 [4, 2048, 2048], P(('groups', 'batch'), 'seq', 'head'), parts along dimension 0
There are 2 independent parts, one for each index of `groups`. A program takes and returns all parts, laid end to end along the dimension named above; each array names one. Nothing has to cross between parts.
All inputs are finite; a program needn't handle non-finite values.
Results may differ from a plain program's by a relative error of at most 0.0034.
Values may be sent and summed in bfloat16 or wider, within the bound.
A program may use at most 64 MiB of HBM per device.

v0:
```python
import math

import jax
import jax.numpy as jnp
import numpy as np
from jax import lax
from jax.sharding import PartitionSpec as P

DK = 16
WINDOW = 64


def from_behind(block, axis, distance):
    devices = range(lax.axis_size(axis))
    route = [(i - distance, i) for i in devices if i - distance in devices]
    return lax.ppermute(block, axis, route)


def prefix(array, axis, join, neutral):
    place = lax.axis_index(axis)
    gathered = jax.tree.map(
        lambda a, kind: lax.all_gather(a.astype(kind), axis), array, (jnp.bfloat16, jnp.bfloat16)
    )
    state = jax.tree.map(lambda a, e: jnp.zeros_like(a) + jnp.asarray(e, a.dtype), array, neutral)

    def one(step, state):
        return join(
            state,
            jax.tree.map(
                lambda a, own: lax.dynamic_index_in_dim(a, step, 0, False).astype(own.dtype),
                gathered,
                array,
            ),
        )

    return lax.fori_loop(0, place, one, state)


def features(vectors):
    upper_rows, upper_cols = np.triu_indices(DK)
    pair_weights = np.where(
        upper_rows == upper_cols, 1.0 / math.sqrt(2.0 * DK), 1.0 / math.sqrt(DK)
    )
    paired = (
        vectors[:, upper_rows]
        * vectors[:, upper_cols]
        * jnp.asarray(pair_weights, dtype=vectors.dtype)
    )
    leading = jnp.ones((vectors.shape[0], 1), vectors.dtype)
    return jnp.concatenate([leading, vectors * DK ** (-0.25), paired], axis=1)


def block_state(key_block, value_block):
    key_feat = features(key_block.astype(jnp.float32)).astype(jnp.bfloat16)
    state_term = jnp.dot(key_feat.T, value_block, preferred_element_type=jnp.float32)
    norm_term = jnp.sum(key_feat.astype(jnp.float32), axis=0)
    return (state_term, norm_term)


def mix_block(
    query_block, key_block, value_block, rim_keys, rim_values, has_prior, prior_state, prior_norm
):
    length = query_block.shape[0]
    rim_width = rim_keys.shape[0]
    tile_rows = min(length, 512)
    ext_keys = jnp.concatenate([rim_keys, key_block], axis=0)
    ext_values = jnp.concatenate([rim_values, value_block], axis=0)
    query_feat = features(query_block.astype(jnp.float32))
    win_scores = jnp.dot(query_block, ext_keys.T, preferred_element_type=jnp.float32) * DK ** (-0.5)
    row_ids = jnp.arange(tile_rows)[:, None]
    col_ids = jnp.arange(rim_width + tile_rows)[None, :]
    visible = (
        (col_ids > row_ids)
        & (col_ids <= row_ids + rim_width)
        & ((col_ids + 0 >= rim_width) | has_prior)
    )
    masked = jnp.where(visible, win_scores, -jnp.inf)
    row_peak = jnp.max(masked, axis=1, keepdims=True)
    raised = jnp.where(visible, jnp.exp(masked - row_peak), 0.0)
    soft_weights = (raised / jnp.sum(raised, axis=1, keepdims=True)).astype(jnp.bfloat16)
    windowed = jnp.dot(soft_weights, ext_values, preferred_element_type=jnp.float32)
    lin_scores = jnp.dot(query_block, key_block.T, preferred_element_type=jnp.float32) * DK ** (
        -0.5
    )
    causal = jnp.arange(tile_rows)[None, :] <= row_ids + 0
    kernel = jnp.where(causal, 1.0 + lin_scores + 0.5 * lin_scores * lin_scores, 0.0).astype(
        jnp.bfloat16
    )
    feat_part = query_feat[0:tile_rows]
    numerator = jnp.dot(kernel, value_block, preferred_element_type=jnp.float32) + jnp.dot(
        feat_part, prior_state, precision=lax.Precision.HIGHEST
    )
    denominator = jnp.sum(kernel.astype(jnp.float32), axis=1) + jnp.dot(
        feat_part, prior_norm, precision=lax.Precision.HIGHEST
    )
    outputs = [windowed + numerator / denominator[:, None]]
    return jnp.concatenate(outputs, axis=0).astype(jnp.bfloat16)


def add_pair(earlier, later):
    return (earlier[0] + later[0], earlier[1] + later[1])


def on_device(queries, key_vectors, value_vectors):
    seq_total = queries.shape[0]
    own_rows = queries.shape[1]
    head_total = queries.shape[2] // DK
    value_width = value_vectors.shape[2] // head_total
    position = lax.axis_index("seq")
    rim_keys, rim_values = from_behind(
        (key_vectors[:, own_rows - WINDOW :, :], value_vectors[:, own_rows - WINDOW :, :]), "seq", 1
    )
    state_list = []
    norm_list = []
    seq_id = 0
    for head_id in range(head_total):
        state_term, norm_term = block_state(
            key_vectors[seq_id, :, head_id * DK : (head_id + 1) * DK],
            value_vectors[seq_id, :, head_id * value_width : (head_id + 1) * value_width],
        )
        state_list.append(state_term)
        norm_list.append(norm_term)
    local_state = jnp.stack(state_list).reshape((seq_total, head_total) + state_list[0].shape)
    local_norm = jnp.stack(norm_list).reshape((seq_total, head_total) + norm_list[0].shape)
    prior_state, prior_norm = prefix(
        (local_state, local_norm),
        "seq",
        add_pair,
        (jnp.zeros_like(local_state), jnp.zeros_like(local_norm)),
    )
    has_prior = position > 0
    seq_id = 0
    head_outputs = []
    for head_id in range(head_total):
        key_slice = slice(head_id * DK, (head_id + 1) * DK)
        value_slice = slice(head_id * value_width, (head_id + 1) * value_width)
        head_outputs.append(
            mix_block(
                queries[seq_id, :, key_slice],
                key_vectors[seq_id, :, key_slice],
                value_vectors[seq_id, :, value_slice],
                rim_keys[seq_id, :, key_slice],
                rim_values[seq_id, :, value_slice],
                has_prior,
                prior_state[seq_id, head_id],
                prior_norm[seq_id, head_id],
            )
        )
    seq_outputs = [jnp.concatenate(head_outputs, axis=1)]
    return jnp.stack(seq_outputs)


def solution(mesh):
    return jax.shard_map(
        on_device,
        mesh=mesh,
        in_specs=(
            P(("groups", "batch"), "seq", "head"),
            P(("groups", "batch"), "seq", "head"),
            P(("groups", "batch"), "seq", "head"),
        ),
        out_specs=P(("groups", "batch"), "seq", "head"),
        check_vma=False,
    )
```

profile of v0, /device:TPU:24, one launch (start us, length us, event | category | flops | bytes accessed | tf_op | source)
XLA Modules:
  0.0 157.7 jit_solution(16398439264313493183)
XLA Ops:
  9.3 1.6 slice.194
  12.1 2.1 %fusion.332 = (bf16[1,512,16]{2,1,0:T(8,128)(2,1)S(1)}, bf16[1,512,16]{2,1,0:T(8,128)(2,1)S(1)}, bf16[1,512,16]{2,1,0:T(8,128)(2,1)S(1)}, bf16[1,512,16]{2,1,0:T...) fusion(bf16[1,512,128]{2,1,0:T(8,128)(2,1)} %param.86), kind=kLoop, calls=%fused_computation.519 | loop fusion | bytes 262144 | tf_op jit(solution)/shard_map/slice | solution.py:118
  22.6 1.5 gather_fusion.8
  24.1 1.5 gather_fusion.9
  27.0 1.5 gather_fusion.7
  28.5 1.5 gather_fusion.4
  30.0 1.5 gather_fusion.5
  31.5 1.5 gather_fusion.2
  35.7 1.5 gather_fusion.30
  38.7 3.3 %multiply_bitcast_fusion = (f32[512,136]{0,1:T(8,128)}, bf16[512,136]{0,1:T(8,128)(2,1)S(1)}, bf16[512,136]{0,1:T(8,128)(2,1)S(1)}, bf16[512,136]{0,1:T(8,128)(2...) fusion(f32[136,512]{1,0:T(8,128)} %gather_fusion.30, ...), kind=kLoop, calls=%fused_computation.201 | loop fusion | flops 1810432 | bytes 6406688 | tf_op jit(solution)/shard_map/mul | solution.py:45
  45.8 1.8 %convert_reduce_fusion = (f32[512]{0:T(512)}, bf16[512,512]{0,1:T(8,128)(2,1)}) fusion(bf16[1,512,128]{2,1,0:T(8,128)(2,1)S(1)} %copy-done, bf16[1,512,128]{2,1,0:T(8,128)(2,1)S(1)} %copy-done.1), kind=kOutput, calls=%fused_computation.144 | convolution fusion | flops 11009536 | bytes 788480 | tf_op jit(solution)/shard_map/dot_general | solution.py:82
  47.6 1.7 %convert_reduce_fusion.7 = (f32[512]{0:T(512)}, bf16[512,512]{0,1:T(8,128)(2,1)}) fusion(bf16[1,512,128]{2,1,0:T(8,128)(2,1)S(1)} %copy-done, bf16[1,512,128]{2,1,0:T(8,128)(2,1)S(1)} %copy-done.1), kind=kOutput, calls=%fused_computation.158 | convolution fusion | flops 11009536 | bytes 788480 | tf_op jit(solution)/shard_map/dot_general | solution.py:82
  49.3 1.8 %convert_reduce_fusion.6 = (f32[512]{0:T(512)}, bf16[512,512]{0,1:T(8,128)(2,1)}) fusion(bf16[1,512,128]{2,1,0:T(8,128)(2,1)S(1)} %copy-done, bf16[1,512,128]{2,1,0:T(8,128)(2,1)S(1)} %copy-done.1), kind=kOutput, calls=%fused_computation.156 | convolution fusion | flops 11009536 | bytes 788480 | tf_op jit(solution)/shard_map/dot_general | solution.py:82
  51.1 1.8 %convert_reduce_fusion.5 = (f32[512]{0:T(512)}, bf16[512,512]{0,1:T(8,128)(2,1)}) fusion(bf16[1,512,128]{2,1,0:T(8,128)(2,1)S(1)} %copy-done, bf16[1,512,128]{2,1,0:T(8,128)(2,1)S(1)} %copy-done.1), kind=kOutput, calls=%fused_computation.154 | convolution fusion | flops 11009536 | bytes 788480 | tf_op jit(solution)/shard_map/dot_general | solution.py:82
  52.9 1.8 %convert_reduce_fusion.4 = (f32[512]{0:T(512)}, bf16[512,512]{0,1:T(8,128)(2,1)}) fusion(bf16[1,512,128]{2,1,0:T(8,128)(2,1)S(1)} %copy-done, bf16[1,512,128]{2,1,0:T(8,128)(2,1)S(1)} %copy-done.1), kind=kOutput, calls=%fused_computation.152 | convolution fusion | flops 11009536 | bytes 788480 | tf_op jit(solution)/shard_map/dot_general | solution.py:82
  54.7 1.8 %convert_reduce_fusion.3 = (f32[512]{0:T(512)}, bf16[512,512]{0,1:T(8,128)(2,1)}) fusion(bf16[1,512,128]{2,1,0:T(8,128)(2,1)S(1)} %copy-done, bf16[1,512,128]{2,1,0:T(8,128)(2,1)S(1)} %copy-done.1), kind=kOutput, calls=%fused_computation.150 | convolution fusion | flops 11009536 | bytes 788480 | tf_op jit(solution)/shard_map/dot_general | solution.py:82
  56.5 1.8 %convert_reduce_fusion.2 = (f32[512]{0:T(512)}, bf16[512,512]{0,1:T(8,128)(2,1)}) fusion(bf16[1,512,128]{2,1,0:T(8,128)(2,1)S(1)} %copy-done, bf16[1,512,128]{2,1,0:T(8,128)(2,1)S(1)} %copy-done.1), kind=kOutput, calls=%fused_computation.148 | convolution fusion | flops 11009536 | bytes 788480 | tf_op jit(solution)/shard_map/dot_general | solution.py:82
  58.3 1.7 %convert_reduce_fusion.1 = (f32[512]{0:T(512)}, bf16[512,512]{0,1:T(8,128)(2,1)}) fusion(bf16[1,512,128]{2,1,0:T(8,128)(2,1)S(1)} %copy-done, bf16[1,512,128]{2,1,0:T(8,128)(2,1)S(1)} %copy-done.1), kind=kOutput, calls=%fused_computation.146 | convolution fusion | flops 11009536 | bytes 788480 | tf_op jit(solution)/shard_map/dot_general | solution.py:82
  65.9 1.9 %fusion.170 = (bf16[153]{0:T(256)(128)(2,1)}, bf16[153]{0:T(256)(128)(2,1)}, bf16[153]{0:T(256)(128)(2,1)}, bf16[153]{0:T(256)(128)(2,1)}, bf16[153]{0:T(256)(12...) fusion(bf16[512,136]{0,1:T(8,128)(2,1)S(1)} %copy-done.31, ...), kind=kLoop, calls=%fused_computation.313 | loop fusion | flops 3837240 | bytes 1247938 | tf_op jit(solution)/shard_map/reduce_sum | solution.py:56
  74.4 1.6 %gather_fusion.20 = f32[136,512]{1,0:T(8,128)} fusion(f32[512,16]{0,1:T(8,128)S(1)} %bitcast_convert_fusion.5, s32[1024]{0:T(1024)} %copy-done.81), kind=kCustom, calls=%fused_computation.20 | custom fusion | bytes 557600 | tf_op jit(solution)/shard_map/gather | solution.py:45
  76.0 1.5 gather_fusion.21
  79.0 1.5 gather_fusion.19
  80.5 1.5 gather_fusion.1
  82.0 1.5 gather_fusion
  84.5 2.1 %fusion.306 = f32[512,128]{0,1:T(8,128)} fusion(bf16[512,512]{0,1:T(8,128)(2,1)} %get-tuple-element.162, bf16[1,512,1024]{2,1,0:T(8,128)(2,1)S(1)} %copy-done.2), kind=kOutput, calls=%fused_computation.501 | convolution fusion | flops 67108864 | bytes 917504 | tf_op jit(solution)/shard_map/dot_general | solution.py:90
  86.6 2.1 %fusion.299 = f32[512,128]{0,1:T(8,128)} fusion(bf16[512,512]{0,1:T(8,128)(2,1)} %get-tuple-element.132, bf16[1,512,1024]{2,1,0:T(8,128)(2,1)S(1)} %copy-done.2), kind=kOutput, calls=%fused_computation.494 | convolution fusion | flops 67108864 | bytes 917504 | tf_op jit(solution)/shard_map/dot_general | solution.py:90
  94.7 2.8 %multiply_bitcast_fusion.1 = (f32[512,136]{0,1:T(8,128)}, f32[512,136]{0,1:T(8,128)}, f32[512,136]{0,1:T(8,128)}, f32[512,136]{0,1:T(8,128)}, f32[512,136]{0,1:T...) fusion(f32[136,512]{1,0:T(8,128)S(1)} %gather_fusion.28, f32[136,512]{1,0:T(8,128)S(1)} %gather_fusion.29, ...), kind=kLoop, calls=%fused_computation.202 | loop fusion | flops 974848 | bytes 5849632 | tf_op jit(solution)/shard_map/mul | solution.py:45
  98.2 15.5 %all_gather.9 = bf16[4,1,8,153]{3,2,1,0:T(8,128)(2,1)S(1)} all-gather(bf16[1,1,8,153]{3,2,1,0:T(8,128)(2,1)S(1)} %stack.74), channel_id=1, replica_groups=mesh['groups'=2,'seq'=4,'head'=2,'batch'=2] {'seq'}, dimensions={0}, use_global_device_ids=true | all-gather | bytes 12240 | tf_op jit(solution)/shard_map/all_gather | solution.py:22
  120.3 2.8 %fusion.65 = (f32[512]{0:T(512)S(1)}, f32[512]{0:T(512)}, f32[512]{0:T(512)}, f32[512]{0:T(512)}, f32[512]{0:T(512)}, /*index=5*/f32[512]{0:T(512)S(1)}, f32[512]{0:T(512)S(1)}, f32[512]{0:T(512)S(1)}) fusion(f32[512,576]{0,1:T(8,128)S(1)} %get-tuple-element.134, f32[512]{0:T(512)S(1)} %get-tuple-element.133, pred[576]{0:T(1024)(128)(4,1)S(1)} %fusion.226, ...), kind=kLoop, calls=%fused_computation.168 | loop fusion | flops 8253440 | bytes 9472576 | tf_op jit(solution)/shard_map/reduce_sum | solution.py:80
  124.1 3.8 %while.12 = (s32[]{:T(128)}, f32[1,8,153,128]{3,2,1,0:T(8,128)S(1)}, f32[1,8,153]{2,1,0:T(8,128)S(1)}, s32[]{:T(128)}, bf16[4,1,8,153,128]{4,2,3,1,0:T(8,128)(2,...) while((s32[]{:T(128)}, f32[1,8,153,128]{3,2,1,0:T(8,128)S(1)}, ...), condition=%wide.region_11.12_spmd, body=%wide.region_10.11_spmd.sunk | while | flops 315797 | bytes 2205791 | solution.py:36
  130.4 1.6 %fusion.18 = f32[512,128]{0,1:T(8,128)S(1)} fusion(f32[512,128]{0,1:T(8,128)} %fusion.306, f32[512,136]{0,1:T(8,128)} %get-tuple-element.115, f32[512,16]{0,1:T(8,128)S(1)} %copy-done.103, f32[153]{0:T(256)} %pad.73.clone, f32[512]{0:T(512)S(1)} %add.317, f32[1,8,153,128]{3,2,1,0:T(8,128)S(1)} %get-tuple-element.39), kind=kOutput, calls=%fused_computation.81 | convolution fusion | flops 120611840 | bytes 920164 | tf_op jit(solution)/shard_map/dot_general | solution.py:90
  148.6 2.3 %copy.121 = bf16[1,512,1024]{2,1,0:T(8,128)(2,1)} copy(bf16[1,512,1024]{1,2,0:T(8,128)(2,1)} %bitcast.431) | data formatting | bytes 2097152 | tf_op jit(solution)/shard_map/stack | solution.py:150
  (444 shorter events, 71.8 us)
Async XLA Ops:
  6.5 117.4 %all-gather.2.cloned.1.call-start = ((), (), s32[]{:S(2)}) async-start(), calls=%async_computation | async-start | bytes 1566720 | tf_op jit(solution)/shard_map/all_gather | solution.py:22
  8.0 105.8 %collective-permute-start = (bf16[1,64,128]{1,2,0:T(8,128)(2,1)}, bf16[1,64,128]{1,2,0:T(8,128)(2,1)}, u32[]{:S(2)}, u32[]{:S(2)}) collective-permute-start(bf16[1,64,128]{1,2,0:T(8,128)(2,1)} %copy.131), channel_id=1, source_target_pairs={{0,4},{4,8},{8,12},{1,5},{5,9},{9,13},{2,6},{6,10},{10,14},{3,7},{... | collective-permute-start | bytes 49160 | tf_op jit(solution)/shard_map/ppermute | solution.py:16
  10.8 112.3 %collective-permute-start.1 = (bf16[1,64,1024]{2,1,0:T(8,128)(2,1)}, bf16[1,64,1024]{2,1,0:T(8,128)(2,1)}, u32[]{:S(2)}, u32[]{:S(2)}) collective-permute-start(bf16[1,64,1024]{2,1,0:T(8,128)(2,1)} %slice.194), channel_id=1, source_target_pairs={{0,4},{4,8},{8,12},{1,5},{5,9},{9,13},{2,6},{6,10},{10,14},{3,7},{... | collective-permute-start | bytes 393224 | tf_op jit(solution)/shard_map/ppermute | solution.py:16
  14.5 27.6 %copy-start.87 = (bf16[512,16]{0,1:T(8,128)(2,1)}, bf16[512,16]{0,1:T(8,128)(2,1)S(1)}, u32[]{:S(2)}) copy-start(bf16[512,16]{0,1:T(8,128)(2,1)S(1)} %get-tuple-element.172) | copy-start | bytes 49156
  14.5 27.8 %copy-start.85 = (bf16[512,16]{0,1:T(8,128)(2,1)}, bf16[512,16]{0,1:T(8,128)(2,1)S(1)}, u32[]{:S(2)}) copy-start(bf16[512,16]{0,1:T(8,128)(2,1)S(1)} %get-tuple-element.171) | copy-start | bytes 49156
  14.7 27.9 %copy-start.91 = (bf16[512,16]{0,1:T(8,128)(2,1)}, bf16[512,16]{0,1:T(8,128)(2,1)S(1)}, u32[]{:S(2)}) copy-start(bf16[512,16]{0,1:T(8,128)(2,1)S(1)} %get-tuple-element.170) | copy-start | bytes 49156
  14.7 28.1 %copy-start.89 = (bf16[512,16]{0,1:T(8,128)(2,1)}, bf16[512,16]{0,1:T(8,128)(2,1)S(1)}, u32[]{:S(2)}) copy-start(bf16[512,16]{0,1:T(8,128)(2,1)S(1)} %get-tuple-element.169) | copy-start | bytes 49156
  15.4 27.8 %copy-start.93 = (bf16[512,16]{0,1:T(8,128)(2,1)}, bf16[512,16]{0,1:T(8,128)(2,1)S(1)}, u32[]{:S(2)}) copy-start(bf16[512,16]{0,1:T(8,128)(2,1)S(1)} %get-tuple-element.168) | copy-start | bytes 49156
  15.4 28.0 %copy-start.92 = (bf16[512,16]{0,1:T(8,128)(2,1)}, bf16[512,16]{0,1:T(8,128)(2,1)S(1)}, u32[]{:S(2)}) copy-start(bf16[512,16]{0,1:T(8,128)(2,1)S(1)} %get-tuple-element.167) | copy-start | bytes 49156
  16.3 55.6 %copy-start.83 = (s32[1024]{0:T(1024)}, s32[1024]{0:T(1024)S(1)}, u32[]{:S(2)}) copy-start(s32[1024]{0:T(1024)S(1)} %get-tuple-element.163) | copy-start | bytes 12292
  16.3 56.4 %copy-start.81 = (s32[1024]{0:T(1024)}, s32[1024]{0:T(1024)S(1)}, u32[]{:S(2)}) copy-start(s32[1024]{0:T(1024)S(1)} %get-tuple-element.164) | copy-start | bytes 12292
  38.7 5.3 %copy-start.134 = (bf16[153]{0:T(256)(128)(2,1)}, bf16[153]{0:T(256)(128)(2,1)S(1)}, u32[]{:S(2)}) copy-start(bf16[153]{0:T(256)(128)(2,1)S(1)} %pad.70.clone) | copy-start | bytes 922
  60.1 5.8 %copy-start.17 = (bf16[512,136]{0,1:T(8,128)(2,1)S(1)}, bf16[512,136]{0,1:T(8,128)(2,1)}, u32[]{:S(2)}) copy-start(bf16[512,136]{0,1:T(8,128)(2,1)} %copy-done.16) | copy-start | bytes 417796
  60.1 5.8 %copy-start.19 = (bf16[512,136]{0,1:T(8,128)(2,1)S(1)}, bf16[512,136]{0,1:T(8,128)(2,1)}, u32[]{:S(2)}) copy-start(bf16[512,136]{0,1:T(8,128)(2,1)} %copy-done.18) | copy-start | bytes 417796
  60.1 5.8 %copy-start.21 = (bf16[512,136]{0,1:T(8,128)(2,1)S(1)}, bf16[512,136]{0,1:T(8,128)(2,1)}, u32[]{:S(2)}) copy-start(bf16[512,136]{0,1:T(8,128)(2,1)} %copy-done.20) | copy-start | bytes 417796
  60.1 5.8 %copy-start.23 = (bf16[512,136]{0,1:T(8,128)(2,1)S(1)}, bf16[512,136]{0,1:T(8,128)(2,1)}, u32[]{:S(2)}) copy-start(bf16[512,136]{0,1:T(8,128)(2,1)} %copy-done.22) | copy-start | bytes 417796
  60.1 5.7 %copy-start.25 = (bf16[512,136]{0,1:T(8,128)(2,1)S(1)}, bf16[512,136]{0,1:T(8,128)(2,1)}, u32[]{:S(2)}) copy-start(bf16[512,136]{0,1:T(8,128)(2,1)} %copy-done.24) | copy-start | bytes 417796
  60.1 5.7 %copy-start.27 = (bf16[512,136]{0,1:T(8,128)(2,1)S(1)}, bf16[512,136]{0,1:T(8,128)(2,1)}, u32[]{:S(2)}) copy-start(bf16[512,136]{0,1:T(8,128)(2,1)} %copy-done.26) | copy-start | bytes 417796
  60.1 5.7 %copy-start.29 = (bf16[512,136]{0,1:T(8,128)(2,1)S(1)}, bf16[512,136]{0,1:T(8,128)(2,1)}, u32[]{:S(2)}) copy-start(bf16[512,136]{0,1:T(8,128)(2,1)} %copy-done.28) | copy-start | bytes 417796
  60.1 5.7 %copy-start.31 = (bf16[512,136]{0,1:T(8,128)(2,1)S(1)}, bf16[512,136]{0,1:T(8,128)(2,1)}, u32[]{:S(2)}) copy-start(bf16[512,136]{0,1:T(8,128)(2,1)} %copy-done.30) | copy-start | bytes 417796
  60.1 5.7 %copy-start.86 = (bf16[512,16]{0,1:T(8,128)(2,1)S(1)}, bf16[512,16]{0,1:T(8,128)(2,1)}, u32[]{:S(2)}) copy-start(bf16[512,16]{0,1:T(8,128)(2,1)} %copy-done.85) | copy-start | bytes 49156
  60.1 5.7 %copy-start.88 = (bf16[512,16]{0,1:T(8,128)(2,1)S(1)}, bf16[512,16]{0,1:T(8,128)(2,1)}, u32[]{:S(2)}) copy-start(bf16[512,16]{0,1:T(8,128)(2,1)} %copy-done.87) | copy-start | bytes 49156
  60.1 5.7 %copy-start.90 = (bf16[512,16]{0,1:T(8,128)(2,1)S(1)}, bf16[512,16]{0,1:T(8,128)(2,1)}, u32[]{:S(2)}) copy-start(bf16[512,16]{0,1:T(8,128)(2,1)} %copy-done.89) | copy-start | bytes 49156
  60.1 5.7 %copy-start.135 = (bf16[153]{0:T(256)(128)(2,1)S(1)}, bf16[153]{0:T(256)(128)(2,1)}, u32[]{:S(2)}) copy-start(bf16[153]{0:T(256)(128)(2,1)} %copy-done.134) | copy-start | bytes 922
  84.5 5.2 %copy-start.33 = (bf16[512,512]{0,1:T(8,128)(2,1)S(1)}, bf16[512,512]{0,1:T(8,128)(2,1)}, u32[]{:S(2)}) copy-start(bf16[512,512]{0,1:T(8,128)(2,1)} %get-tuple-element.152) | copy-start | bytes 1572868
  94.7 19.8 %copy-start.72 = (bf16[1,512,16]{1,2,0:T(8,128)(2,1)S(1)}, bf16[1,512,16]{1,2,0:T(8,128)(2,1)}, u32[]{:S(2)}) copy-start(bf16[1,512,16]{1,2,0:T(8,128)(2,1)} %copy-done.71) | copy-start | bytes 49156
  94.7 19.8 %copy-start.104 = (s32[512]{0:T(512)S(1)}, s32[512]{0:T(512)}, u32[]{:S(2)}) copy-start(s32[512]{0:T(512)} %iota_add_fusion) | copy-start | bytes 6148
  97.5 22.7 %copy-start.129 = (pred[576]{0:T(1024)(128)(4,1)}, pred[576]{0:T(1024)(128)(4,1)S(1)}, u32[]{:S(2)}) copy-start(pred[576]{0:T(1024)(128)(4,1)S(1)} %fusion.226) | copy-start | bytes 1732
  124.1 5.2 %copy-start.113 = (f32[512]{0:T(512)S(1)}, f32[512]{0:T(512)}, u32[]{:S(2)}) copy-start(f32[512]{0:T(512)} %get-tuple-element.161) | copy-start | bytes 6148
  124.1 5.2 %copy-start.51 = (f32[512,136]{0,1:T(8,128)S(1)}, f32[512,136]{0,1:T(8,128)}, u32[]{:S(2)}) copy-start(f32[512,136]{0,1:T(8,128)} %get-tuple-element.124) | copy-start | bytes 835588
  124.1 5.2 %copy-start.102 = (f32[512,16]{0,1:T(8,128)S(1)}, f32[512,16]{0,1:T(8,128)}, u32[]{:S(2)}) copy-start(f32[512,16]{0,1:T(8,128)} %broadcast_multiply_fusion.1) | copy-start | bytes 98308
  124.1 6.2 %copy-start.114 = (f32[512]{0:T(512)S(1)}, f32[512]{0:T(512)}, u32[]{:S(2)}) copy-start(f32[512]{0:T(512)} %get-tuple-element.159) | copy-start | bytes 6148
  (115 other events, 226.5 us)
Sparse Core Ops, SparseCore 0:
  45.3 33.1 all-gather.1
where the time goes:
time: 160 us; the launch traced here: 158 us
  local copies, waits for them, and re-layouts  60.8 us (38%)
  matrix products  45.4 us (28%)
  other arithmetic  17.7 us (11%)
  blocking collectives  15.5 us (10%)
  between operations  15.4 us (10%)
  starting transfers between devices  2.56 us (2%)
    gather x16, local copies, waits for them, and re-layouts, features(): vectors[:, upper_rows] * vectors[:, upper_cols]  18.4 us
    gather x16, local copies, waits for them, and re-layouts, features(): vectors[:, upper_cols]  18.2 us
    all_gather x1, blocking collectives, prefix(): lax.all_gather(a.astype(kind), axis)  15.5 us
    dot_general x8, matrix products, mix_block(): jnp.dot(query_block, key_block.T, preferred_element_type=jnp.float32)  14.2 us
    dot_general x8, matrix products, mix_block(): jnp.dot(kernel, value_block, preferred_element_type=jnp.float32)  10.1 us
    unnamed x305, local copies, waits for them, and re-layouts  9.24 us
    mul x2, other arithmetic, features(): vectors[:, upper_rows] * vectors[:, upper_cols]  6.04 us
    dot_general x8, matrix products, mix_block(): jnp.dot(feat_part, prior_state, precision=lax.Precision.HIGHEST)  5.56 us
  transfers between devices with their start and end apart: 3, of which 0 were waited for; matrix products, arithmetic and copies ran while one was open for 60% of the time, Pallas kernels for 0%

commit v1 on v0

v1 whole, which is shorter than its diff:
```python
import jax
import jax.numpy as jnp
from jax import lax
from jax.experimental import pallas as pl
from jax.experimental.pallas import tpu as pltpu
from jax.sharding import PartitionSpec as P

DK = 16
DV = 128
WINDOW = 64
ROWS = 160
KEY_SUM_ROW = 137
LANES = 128
BLOCK = 256
SLOT = 32
BF16 = jnp.bfloat16
F32 = jnp.float32
MESH = pl.DeviceIdType.MESH


def iota(shape, dim):
    return lax.broadcasted_iota(jnp.int32, shape, dim)


def dot(a, b):
    return jnp.dot(a, b, preferred_element_type=F32)


def dot_nt(a, b):
    return lax.dot_general(a, b, (((1,), (1,)), ((), ())), preferred_element_type=F32)


def rolled_picker(distance, width):
    shape = (width, width)
    row, col = iota(shape, 0), iota(shape, 1)
    part = row % DK
    target = row - part + (part + distance) % DK
    hit = row * 0 + target == col
    if distance == DK // 2:
        hit = hit & (part < DK // 2)
    return jnp.where(hit, 1.0 if distance == 0 else 0.25, 0.0).astype(BF16)


def pair_picker(heads):
    above = DK * (heads - 1)
    shape = (above + DK * heads, 2 * LANES)
    row, col = iota(shape, 0) - above, iota(shape, 1)
    part, turn = col % DK, (col % LANES) // DK
    right = col >= LANES
    hit = row == jnp.where(right, (part + turn) % DK, part)
    weight = jnp.where(right, jnp.where(turn == 0, 0.0625, 0.5), 1.0)
    return jnp.where(hit, weight, 0.0).astype(BF16)


def tail_picker(group, heads):
    shape = (DK * heads, 2 * LANES)
    row, col = iota(shape, 0), iota(shape, 1)
    slot, at = (col % LANES) // SLOT, col % SLOT
    base = DK * (4 * group + slot)
    right = col >= LANES
    half = DK // 2
    left_hit = ((at < half) & (row == base + at)) | ((at >= DK) & (row == base + at - DK))
    right_hit = (at < half) & (row == base + at + half)
    picked = jnp.where(right, jnp.where(right_hit, 0.5, 0.0), jnp.where(left_hit, 1.0, 0.0))
    return picked.astype(BF16)


def kernel(
    n, heads,
    q_hbm, k_hbm, v_hbm, out_ref,
    q, kx, vx, phi_k, own, sent, prior, picker, tails, phi_q, sums, win,
    load_sem, rim_send, rim_recv, send_sem, recv_sem,
):
    rows = q.shape[0]
    width = q.shape[1]
    groups = tails.shape[0]
    place = lax.axis_index("seq")
    has_prior = place > 0
    has_next = place < n - 1
    half = LANES // 2

    loads = [
        pltpu.make_async_copy(k_hbm.at[0], kx.at[pl.ds(LANES, rows)], load_sem.at[0]),
        pltpu.make_async_copy(v_hbm.at[0], vx.at[pl.ds(LANES, rows)], load_sem.at[1]),
        pltpu.make_async_copy(q_hbm.at[0], q, load_sem.at[2]),
    ]
    for load in loads:
        load.start()

    barrier = pltpu.get_barrier_semaphore()

    @pl.when(has_prior)
    def _():
        pl.semaphore_signal(barrier, inc=1, device_id={"seq": place - 1}, device_id_type=MESH)

    rim = [
        pltpu.make_async_remote_copy(
            src_ref=src.at[0, pl.ds(rows - WINDOW, WINDOW)],
            dst_ref=dst.at[pl.ds(half, WINDOW)],
            send_sem=rim_send.at[i],
            recv_sem=rim_recv.at[i],
            device_id={"seq": place + 1},
            device_id_type=MESH,
        )
        for i, (src, dst) in enumerate(((k_hbm, kx), (v_hbm, vx)))
    ]

    def chunk(h):
        return pltpu.make_async_remote_copy(
            src_ref=sent.at[h],
            dst_ref=prior.at[h],
            send_sem=send_sem.at[h],
            recv_sem=recv_sem.at[h],
            device_id={"seq": place + 1},
            device_id_type=MESH,
        )

    @pl.when(has_next)
    def _():
        pl.semaphore_wait(barrier, 1)
        for copy in rim:
            copy.start()

    kx[0:half] = jnp.zeros((half, width), BF16)
    vx[0:half] = jnp.zeros((half, vx.shape[1]), BF16)

    @pl.when(jnp.logical_not(has_prior))
    def _():
        kx[half:LANES] = jnp.zeros((half, width), BF16)
        vx[half:LANES] = jnp.zeros((half, vx.shape[1]), BF16)
        prior[...] = jnp.zeros(prior.shape, BF16)

    picker[...] = pair_picker(heads)
    loads[0].wait()

    keys = kx[LANES:LANES + rows]
    plain = dot_nt(rolled_picker(0, width), keys)

    def put(group, block):
        block = block.astype(BF16)
        for h in range(heads):
            phi_k[h, group * DK:(group + 1) * DK, :] = block[h * DK:(h + 1) * DK]

    put(0, plain * plain)
    for distance in range(1, DK // 2 + 1):
        other = dot_nt(rolled_picker(distance, width), keys)
        product = plain * other
        if distance == DK // 2:
            one = jnp.where(iota((width, 1), 0) % DK == DK // 2, 1.0, 0.0)
            product = product + one
        put(distance, product)
    put(DK // 2 + 1, plain * 0.5)

    ones = jnp.ones((BLOCK, DV), BF16)

    def with_ones(values):
        return jnp.concatenate([values, jnp.ones((values.shape[0], DV), BF16)], axis=1)

    loads[1].wait()

    def state(h, carry):
        lanes = pl.ds(pl.multiple_of(h * DV, DV), DV)
        full = dot(phi_k[h], with_ones(vx[LANES:LANES + rows, lanes]))
        eye = iota((LANES, LANES), 0) == iota((LANES, LANES), 1)
        key_sums = full[:, DV:]
        low = jnp.sum(jnp.where(eye, key_sums[:LANES], 0.0), axis=0, keepdims=True)
        high = jnp.sum(
            jnp.where(eye[:ROWS - LANES], key_sums[LANES:], 0.0), axis=0, keepdims=True
        )
        row = iota((ROWS, DV), 0)
        term = jnp.where(
            row == KEY_SUM_ROW, low, jnp.where(row == KEY_SUM_ROW + 1, high, full[:, :DV])
        )
        own[h] = term

        @pl.when(jnp.logical_not(has_prior) & has_next)
        def _():
            sent[h] = term.astype(BF16)
            chunk(h).start()

        return carry

    lax.fori_loop(0, heads, state, 0)

    loads[2].wait()
    for group in range(groups):
        both = dot(q[...], tail_picker(group, heads))
        at = iota((1, LANES), 1) % SLOT
        left = both[:, :LANES] + jnp.where(at == DK // 2, 2.0, 0.0)
        right = both[:, LANES:] + jnp.where((at == DK // 2) | (at >= DK), 1.0, 0.0)
        tails[group] = (left * right).astype(BF16)

    @pl.when(has_prior)
    def _():
        for copy in rim:
            copy.wait_recv()

    def local(h):
        lanes = pl.ds(pl.multiple_of(h * DV, DV), DV)
        scale = jnp.where(iota((1, width), 1) // DK == h, 0.25, 0.0).astype(BF16)
        row = iota((LANES, LANES), 0)
        col = iota((LANES, LANES), 1)
        near = (col <= row) & (row - col < WINDOW)
        far = (col > row + half)[:half]
        for big in range(rows // BLOCK):
            start = big * BLOCK
            until = start + BLOCK
            queries = q[start:until] * scale
            scores = dot_nt(queries, kx[LANES:LANES + until])
            raised = scores + 1.0
            weights = raised * raised + 1.0
            causal = iota((BLOCK, BLOCK), 1) <= iota((BLOCK, BLOCK), 0)
            diagonal = jnp.where(causal, weights[:, start:], 0.0)
            if big:
                weights = jnp.concatenate([weights[:, :start], diagonal], axis=1)
            else:
                weights = diagonal
            sums[h, start:until] = dot(
                weights.astype(BF16), with_ones(vx[LANES:LANES + until, lanes])
            )
            for small in range(BLOCK // LANES):
                begin = start + small * LANES
                part = scores[small * LANES:(small + 1) * LANES]
                here = part[:, begin:begin + LANES]
                if begin:
                    before = part[:half, begin - LANES:begin]
                    seen = far
                else:
                    before = dot_nt(queries[:half], kx[0:LANES])
                    seen = far & has_prior
                here = jnp.where(near, here, -jnp.inf)
                before = jnp.where(seen, before, -jnp.inf)
                top = jnp.max(jnp.maximum(here[:half], before), axis=1, keepdims=True)
                low = jnp.max(here[half:], axis=1, keepdims=True)
                shares = jnp.concatenate(
                    [
                        jnp.concatenate(
                            [jnp.exp(before - top), jnp.zeros((half, LANES), F32)], axis=0
                        ),
                        jnp.exp(here - jnp.concatenate([top, low], axis=0)),
                    ],
                    axis=1,
                ).astype(BF16)
                both = dot(shares, with_ones(vx[begin:begin + 2 * LANES, lanes]))
                win[h, begin:begin + LANES] = both[:, :DV] / both[:, DV:]
        pick = picker[pl.ds(pl.multiple_of(DK * (heads - 1 - h), DK), width)]
        both = dot(q[...], pick)
        phi_q[h] = (both[:, :LANES] * both[:, LANES:]).astype(BF16)

    def finish(h):
        @pl.when(has_prior)
        def _():
            chunk(h).wait_recv()

            @pl.when(has_next)
            def _():
                sent[h] = (prior[h].astype(F32) + own[h]).astype(BF16)
                chunk(h).start()

        lanes = pl.ds(pl.multiple_of(h * DV, DV), DV)
        before = prior[h]
        eye = iota((LANES, LANES), 0) == iota((LANES, LANES), 1)
        wide = before[DK * 8:DK * 9].astype(F32)
        at = KEY_SUM_ROW - DK * 8
        low, high = wide[at:at + 1], wide[at + 1:at + 2]
        diagonal = jnp.concatenate(
            [jnp.where(eye, low, 0.0), jnp.where(eye[:SLOT], high, 0.0)], axis=0
        ).astype(BF16)
        key_sums = dot(diagonal, jnp.ones((LANES, DV), BF16)).astype(BF16)
        state = jnp.concatenate([before, key_sums], axis=1)
        tail = jnp.concatenate([state[LANES:]] * (LANES // SLOT), axis=0)
        slot = iota((LANES, 1), 0) // SLOT
        tail = jnp.where(slot == h % 4, tail, jnp.zeros_like(tail))
        state = jnp.concatenate([state[:LANES], tail], axis=0)
        feats = jnp.concatenate([phi_q[h], tails[h // 4]], axis=1)
        total = sums[h] + dot(feats, state)
        out_ref[0, :, lanes] = (win[h] + total[:, :DV] / total[:, DV:]).astype(BF16)

    lag = jnp.minimum(2 * jnp.maximum(place - 1, 0), heads)

    def step(t, carry):
        @pl.when(t < heads)
        def _():
            local(t)

        @pl.when((t >= lag) & (t < lag + heads))
        def _():
            finish(t - lag)

        return carry

    lax.fori_loop(0, 2 * heads, step, 0)

    @pl.when(has_next)
    def _():
        for copy in rim:
            copy.wait_send()

        def drain(h, carry):
            chunk(h).wait_send()
            return carry

        lax.fori_loop(0, heads, drain, 0)


def on_device(queries, key_vectors, value_vectors):
    n = lax.axis_size("seq")
    rows, width = queries.shape[1:]
    heads = width // DK
    values = value_vectors.shape[2]
    groups = -(-heads // 4)
    any_space = pl.BlockSpec(memory_space=pl.ANY)

    def body(*refs):
        kernel(n, heads, *refs)

    return pl.pallas_call(
        body,
        out_shape=jax.ShapeDtypeStruct((1, rows, values), BF16),
        in_specs=[any_space] * 3,
        out_specs=pl.BlockSpec(memory_space=pltpu.VMEM),
        scratch_shapes=[
            pltpu.VMEM((rows, width), BF16),
            pltpu.VMEM((LANES + rows, width), BF16),
            pltpu.VMEM((LANES + rows, values), BF16),
            pltpu.VMEM((heads, ROWS, rows), BF16),
            pltpu.VMEM((heads, ROWS, DV), F32),
            pltpu.VMEM((heads, ROWS, DV), BF16),
            pltpu.VMEM((heads, ROWS, DV), BF16),
            pltpu.VMEM((DK * (2 * heads - 1), 2 * LANES), BF16),
            pltpu.VMEM((groups, rows, LANES), BF16),
            pltpu.VMEM((heads, rows, LANES), BF16),
            pltpu.VMEM((heads, rows, 2 * DV), F32),
            pltpu.VMEM((heads, rows, DV), F32),
            pltpu.SemaphoreType.DMA((3,)),
            pltpu.SemaphoreType.DMA((2,)),
            pltpu.SemaphoreType.DMA((2,)),
            pltpu.SemaphoreType.DMA((heads,)),
            pltpu.SemaphoreType.DMA((heads,)),
        ],
        compiler_params=pltpu.CompilerParams(
            collective_id=0, has_side_effects=True, vmem_limit_bytes=48 * 2**20
        ),
    )(queries, key_vectors, value_vectors)


def solution(mesh):
    spec = P(("groups", "batch"), "seq", "head")
    return jax.shard_map(
        on_device, mesh=mesh, in_specs=(spec, spec, spec), out_specs=spec, check_vma=False
    )
```

time: 160 us -> 28.3 us (0.18); the launches traced: 158 us -> 28.2 us
  local copies, waits for them, and re-layouts: 60.8 us -> 4 us
  matrix products: 45.4 us -> 0 us
  Pallas kernels: 0 us -> 24.1 us
  other arithmetic: 17.7 us -> 0 us
  blocking collectives: 15.5 us -> 0 us
  between operations: 15.4 us -> 0.01 us
  starting transfers between devices: 2.56 us -> 0 us
    dot_general x56 -> x0, matrix products: 45.4 us -> none  [the longest x8 14.2 us: mix_block(): jnp.dot(query_block, key_block.T, preferred_element_type=jnp.float32)]
    gather x32 -> x0, local copies, waits for them, and re-layouts: 36.5 us -> none  [the longest x16 18.4 us: features(): vectors[:, upper_rows] * vectors[:, upper_cols]]
    pallas_call x0 -> x1, Pallas kernels: none -> 24.1 us  [on_device(): pl.pallas_call(body, out_shape=jax.ShapeDtypeStruct((1, rows, values), BF...]
    all_gather x1 -> x0, blocking collectives: 15.5 us -> none  [prefix(): lax.all_gather(a.astype(kind), axis)]
    mul x10 -> x0, other arithmetic: 11.1 us -> none  [the longest x2 6.04 us: features(): vectors[:, upper_rows] * vectors[:, upper_cols]]
    slice x4 -> x0, local copies, waits for them, and re-layouts: 5.63 us -> none  [the longest x1 2.12 us: on_device(): key_vectors[seq_id, :, head_id * DK:(head_id + 1) * DK]]
    unnamed x305 -> x7, local copies, waits for them, and re-layouts: 9.24 us -> 4 us
    reduce_sum x2 -> x0, other arithmetic: 4.76 us -> none  [the longest x1 2.84 us: mix_block(): jnp.sum(raised, axis=1, keepdims=True)]
  transfers between devices with their start and end apart: 3 -> 0, of which waited for: 0 -> 0; matrix products, arithmetic and copies ran while one was open for 60% -> 0% of each run, Pallas kernels for 0% -> 0%
where the time goes in v1:
time: 28.3 us; the launch traced here: 28.2 us
  Pallas kernels  24.1 us (85%)
  local copies, waits for them, and re-layouts  4 us (14%)
    pallas_call x1, Pallas kernels, on_device(): pl.pallas_call(body, out_shape=jax.ShapeDtypeStruct((1, rows, values), BF...  24.1 us
    unnamed x7, local copies, waits for them, and re-layouts  4 us

profile of v1, /device:TPU:24, one launch (start us, length us, event | category | flops | bytes accessed | tf_op | source)
XLA Modules:
  0.0 28.2 jit_solution(13365305113422683638)
XLA Ops:
  0.0 0.0 copy-start
  0.0 1.2 %copy-done = bf16[1,512,1024]{2,1,0:T(8,128)(2,1)S(1)} copy-done((bf16[1,512,1024]{2,1,0:T(8,128)(2,1)S(1)}, bf16[1,512,1024]{2,1,0:T(8,128)(2,1)}, u32[]{:S(2)}) %copy-start) | copy-done | bytes 1048600
  1.2 0.0 copy-start.1
  1.2 0.9 %copy-done.1 = bf16[1,512,128]{2,1,0:T(8,128)(2,1)S(1)} copy-done((bf16[1,512,128]{2,1,0:T(8,128)(2,1)S(1)}, bf16[1,512,128]{2,1,0:T(8,128)(2,1)}, u32[]{:S(2)}) %copy-start.1) | copy-done | bytes 131096
  2.1 0.0 copy-start.2
  2.1 0.9 %copy-done.2 = bf16[1,512,128]{2,1,0:T(8,128)(2,1)S(1)} copy-done((bf16[1,512,128]{2,1,0:T(8,128)(2,1)S(1)}, bf16[1,512,128]{2,1,0:T(8,128)(2,1)}, u32[]{:S(2)}) %copy-start.2) | copy-done | bytes 131096
  3.0 24.1 %shard_map.37 = bf16[1,512,1024]{2,1,0:T(8,128)(2,1)S(1)} custom-call(bf16[1,512,128]{2,1,0:T(8,128)(2,1)S(1)} %copy-done.1, bf16[1,512,128]{2,1,0:T(8,128)(2,1)S(1)} %copy-done.2, bf16[1,512,1024]{2,1,0:T(8,128)(2,1)S(1)} %copy-done), custom_call_target="tpu_custom_call" | custom-call | tf_op jit(solution)/shard_map/pallas_call | solution.py:317
  27.2 1.0 %copy.5 = bf16[1,512,1024]{2,1,0:T(8,128)(2,1)} copy(bf16[1,512,1024]{2,1,0:T(8,128)(2,1)S(1)} %shard_map.37) | data formatting | bytes 2097152
Async XLA Ops:
  0.0 1.2 %copy-start = (bf16[1,512,1024]{2,1,0:T(8,128)(2,1)S(1)}, bf16[1,512,1024]{2,1,0:T(8,128)(2,1)}, u32[]{:S(2)}) copy-start(bf16[1,512,1024]{2,1,0:T(8,128)(2,1)} %refs_2_.1) | copy-start | bytes 3145732
  1.2 0.9 %copy-start.1 = (bf16[1,512,128]{2,1,0:T(8,128)(2,1)S(1)}, bf16[1,512,128]{2,1,0:T(8,128)(2,1)}, u32[]{:S(2)}) copy-start(bf16[1,512,128]{2,1,0:T(8,128)(2,1)} %refs_0_.1) | copy-start | bytes 393220
  2.1 0.9 %copy-start.2 = (bf16[1,512,128]{2,1,0:T(8,128)(2,1)S(1)}, bf16[1,512,128]{2,1,0:T(8,128)(2,1)}, u32[]{:S(2)}) copy-start(bf16[1,512,128]{2,1,0:T(8,128)(2,1)} %refs_1_.1) | copy-start | bytes 393220

commit v2 on v1

v2 whole, which is shorter than its diff:
```python
import jax
import jax.numpy as jnp
from jax import lax
from jax.experimental import pallas as pl
from jax.experimental.pallas import tpu as pltpu
from jax.sharding import PartitionSpec as P

DK = 16
DV = 128
WINDOW = 64
ROWS = 160
KEY_SUM_ROW = 137
LANES = 128
BLOCK = 256
SLOT = 32
BF16 = jnp.bfloat16
F32 = jnp.float32
MESH = pl.DeviceIdType.MESH


def iota(shape, dim):
    return lax.broadcasted_iota(jnp.int32, shape, dim)


def dot(a, b):
    return jnp.dot(a, b, preferred_element_type=F32)


def inverse(x):
    guess = pl.reciprocal(x, approx=True)
    return guess * (2.0 - x * guess)


def dot_nt(a, b):
    return lax.dot_general(a, b, (((1,), (1,)), ((), ())), preferred_element_type=F32)


def rolled_picker(distance, width):
    shape = (width, width)
    row, col = iota(shape, 0), iota(shape, 1)
    part = row & (DK - 1)
    target = row - part + ((part + distance) & (DK - 1))
    hit = target == col
    if distance == DK // 2:
        hit = hit & (part < DK // 2)
    return jnp.where(hit, 1.0 if distance == 0 else 0.25, 0.0).astype(BF16)


def pair_picker(heads):
    above = DK * (heads - 1)
    shape = (above + DK * heads, 2 * LANES)
    row, col = iota(shape, 0) - above, iota(shape, 1)
    part, turn = col & (DK - 1), (col & (LANES - 1)) >> 4
    right = col >= LANES
    hit = row == jnp.where(right, (part + turn) & (DK - 1), part)
    weight = jnp.where(right, jnp.where(turn == 0, 0.0625, 0.5), 1.0)
    return jnp.where(hit, weight, 0.0).astype(BF16)


def tail_picker(group, heads):
    shape = (DK * heads, 2 * LANES)
    row, col = iota(shape, 0), iota(shape, 1)
    slot, at = (col & (LANES - 1)) >> 5, col & (SLOT - 1)
    base = DK * (4 * group + slot)
    right = col >= LANES
    half = DK // 2
    left_hit = ((at < half) & (row == base + at)) | ((at >= DK) & (row == base + at - DK))
    right_hit = (at < half) & (row == base + at + half)
    picked = jnp.where(right, jnp.where(right_hit, 0.5, 0.0), jnp.where(left_hit, 1.0, 0.0))
    return picked.astype(BF16)


def kernel(
    n, heads,
    q_hbm, k_hbm, v_hbm, out_ref,
    q, kx, vx, phi_k, own, sent, prior, picker, tails, phi_q, sums, win,
    load_sem, rim_send, rim_recv, send_sem, recv_sem,
):
    rows = q.shape[0]
    width = q.shape[1]
    groups = tails.shape[0]
    place = lax.axis_index("seq")
    has_prior = place > 0
    has_next = place < n - 1
    half = LANES // 2

    loads = [
        pltpu.make_async_copy(k_hbm.at[0], kx.at[pl.ds(LANES, rows)], load_sem.at[0]),
        pltpu.make_async_copy(v_hbm.at[0], vx.at[pl.ds(LANES, rows)], load_sem.at[1]),
        pltpu.make_async_copy(q_hbm.at[0], q, load_sem.at[2]),
    ]
    for load in loads:
        load.start()

    barrier = pltpu.get_barrier_semaphore()

    @pl.when(has_prior)
    def _():
        pl.semaphore_signal(barrier, inc=1, device_id={"seq": place - 1}, device_id_type=MESH)

    rim = [
        pltpu.make_async_remote_copy(
            src_ref=src.at[0, pl.ds(rows - WINDOW, WINDOW)],
            dst_ref=dst.at[pl.ds(half, WINDOW)],
            send_sem=rim_send.at[i],
            recv_sem=rim_recv.at[i],
            device_id={"seq": place + 1},
            device_id_type=MESH,
        )
        for i, (src, dst) in enumerate(((k_hbm, kx), (v_hbm, vx)))
    ]

    def chunk(h):
        return pltpu.make_async_remote_copy(
            src_ref=sent.at[h],
            dst_ref=prior.at[h],
            send_sem=send_sem.at[h],
            recv_sem=recv_sem.at[h],
            device_id={"seq": place + 1},
            device_id_type=MESH,
        )

    @pl.when(has_next)
    def _():
        pl.semaphore_wait(barrier, 1)
        for copy in rim:
            copy.start()

    kx[0:half] = jnp.zeros((half, width), BF16)
    vx[0:half] = jnp.zeros((half, vx.shape[1]), BF16)

    @pl.when(jnp.logical_not(has_prior))
    def _():
        kx[half:LANES] = jnp.zeros((half, width), BF16)
        vx[half:LANES] = jnp.zeros((half, vx.shape[1]), BF16)
        prior[...] = jnp.zeros(prior.shape, BF16)

    loads[0].wait()

    keys = kx[LANES:LANES + rows]
    plain = dot_nt(rolled_picker(0, width), keys)

    def put(group, block):
        block = block.astype(BF16)
        for h in range(heads):
            phi_k[h, group * DK:(group + 1) * DK, :] = block[h * DK:(h + 1) * DK]

    put(0, plain * plain)
    for distance in range(1, DK // 2 + 1):
        other = dot_nt(rolled_picker(distance, width), keys)
        product = plain * other
        if distance == DK // 2:
            one = jnp.where(iota((width, 1), 0) & (DK - 1) == DK // 2, 1.0, 0.0)
            product = product + one
        put(distance, product)
    put(DK // 2 + 1, plain * 0.5)

    def with_ones(values):
        return jnp.concatenate([values, jnp.ones((values.shape[0], DV), BF16)], axis=1)

    loads[1].wait()

    def state(h):
        full = dot(phi_k[h], with_ones(vx[LANES:LANES + rows, h * DV:(h + 1) * DV]))
        eye = iota((LANES, LANES), 0) == (iota((LANES, LANES), 1))
        key_sums = full[:, DV:]
        low = jnp.sum(jnp.where(eye, key_sums[:LANES], 0.0), axis=0, keepdims=True)
        hit = iota((SLOT, LANES), 0) == (iota((SLOT, LANES), 1) & (SLOT - 1))
        high = jnp.sum(jnp.where(hit, key_sums[LANES:], 0.0), axis=0, keepdims=True)
        row = iota((ROWS, DV), 0)
        own[h] = jnp.where(
            row == KEY_SUM_ROW, low, jnp.where(row == KEY_SUM_ROW + 1, high, full[:, :DV])
        )

    pair = 2 - heads % 2
    for first in range(0, heads, pair):
        for h in range(first, first + pair):
            state(h)

        @pl.when(jnp.logical_not(has_prior) & has_next)
        def _():
            for h in range(first, first + pair):
                sent[h] = own[h].astype(BF16)
                chunk(h).start()

    picker[...] = pair_picker(heads)
    loads[2].wait()
    for group in range(groups):
        both = dot(q[...], tail_picker(group, heads))
        at = iota((1, LANES), 1) & (SLOT - 1)
        left = both[:, :LANES] + jnp.where(at == DK // 2, 2.0, 0.0)
        right = both[:, LANES:] + jnp.where((at == DK // 2) | (at >= DK), 1.0, 0.0)
        tails[group] = (left * right).astype(BF16)

    @pl.when(has_prior)
    def _():
        for copy in rim:
            copy.wait_recv()

    def local(h, big):
        lanes = pl.ds(pl.multiple_of(h * DV, DV), DV)
        scale = jnp.where(iota((1, width), 1) >> 4 == h, 0.25, 0.0).astype(BF16)
        row = iota((LANES, LANES), 0)
        col = iota((LANES, LANES), 1)
        near = (col <= row) & (row - col < WINDOW)
        far = (col > row + half)[:half]
        start = big * BLOCK
        until = start + BLOCK
        queries = q[start:until] * scale
        scores = dot_nt(queries, kx[LANES:LANES + until])
        raised = scores + 1.0
        weights = raised * raised + 1.0
        causal = iota((BLOCK, BLOCK), 1) <= iota((BLOCK, BLOCK), 0)
        diagonal = jnp.where(causal, weights[:, start:], 0.0)
        if big:
            weights = jnp.concatenate([weights[:, :start], diagonal], axis=1)
        else:
            weights = diagonal
        sums[h, start:until] = dot(
            weights.astype(BF16), with_ones(vx[LANES:LANES + until, lanes])
        )
        for small in range(BLOCK // LANES):
            begin = start + small * LANES
            part = scores[small * LANES:(small + 1) * LANES]
            here = part[:, begin:begin + LANES]
            if begin:
                before = part[:half, begin - LANES:begin]
                seen = far
            else:
                before = dot_nt(queries[:half], kx[0:LANES])
                seen = far & has_prior
            here = jnp.where(near, here, -jnp.inf)
            before = jnp.where(seen, before, -jnp.inf)
            top = jnp.max(jnp.maximum(here[:half], before), axis=1, keepdims=True)
            low = jnp.max(here[half:], axis=1, keepdims=True)
            shares = jnp.concatenate(
                [
                    jnp.concatenate(
                        [jnp.exp(before - top), jnp.zeros((half, LANES), F32)], axis=0
                    ),
                    jnp.exp(here - jnp.concatenate([top, low], axis=0)),
                ],
                axis=1,
            ).astype(BF16)
            both = dot(shares, with_ones(vx[begin:begin + 2 * LANES, lanes]))
            win[h, begin:begin + LANES] = both[:, :DV] * inverse(both[:, DV:])
        pick = picker[pl.ds(pl.multiple_of(DK * (heads - 1 - h), DK), width)]
        both = dot(q[start:until], pick)
        phi_q[h, start:until] = (both[:, :LANES] * both[:, LANES:]).astype(BF16)

    def forward(h):
        chunk(h).wait_recv()

        @pl.when(has_next)
        def _():
            sent[h] = (prior[h].astype(F32) + own[h]).astype(BF16)
            chunk(h).start()

    def finish(h):
        lanes = pl.ds(pl.multiple_of(h * DV, DV), DV)
        before = prior[h]
        wide = before[DK * 8:DK * 9].astype(F32)
        at = KEY_SUM_ROW - DK * 8
        lane = iota((1, LANES), 1)
        high = jnp.where(lane >> 5 == (h & 3), wide[at + 1:at + 2], 0.0)
        key_sums = jnp.concatenate([wide[at:at + 1], high], axis=1).astype(BF16)
        key_sums = jnp.broadcast_to(key_sums, (DV, 2 * LANES))
        tail = jnp.concatenate([before[LANES:]] * (LANES // SLOT), axis=0)
        slot = iota((LANES, 1), 0) >> 5
        tail = jnp.where(slot == (h & 3), tail, jnp.zeros_like(tail))
        state = jnp.concatenate([before[:LANES], tail], axis=0)
        feats = jnp.concatenate([phi_q[h], tails[h >> 2]], axis=1)
        total = sums[h, :, :DV] + dot(feats, state)
        weight = sums[h, :, DV:] + dot_nt(feats, key_sums)
        out_ref[0, :, lanes] = (win[h] + total * inverse(weight)).astype(BF16)

    blocks = rows // BLOCK
    late = jnp.minimum(jnp.maximum(place - 1, 0), heads // 2)
    receive_lag = 4 * late + 1
    finish_lag = 2 * late

    def step(t, carry):
        for big in range(blocks):
            @pl.when(t < heads)
            def _():
                local(t, big)

            arriving = blocks * t + big - receive_lag

            @pl.when(has_prior & (arriving >= 0) & (arriving < heads))
            def _():
                forward(arriving)

        @pl.when((t >= finish_lag) & (t < finish_lag + heads))
        def _():
            finish(t - finish_lag)

        return carry

    lax.fori_loop(0, 2 * heads, step, 0)

    @pl.when(has_next)
    def _():
        for copy in rim:
            copy.wait_send()

        def drain(h, carry):
            chunk(h).wait_send()
            return carry

        lax.fori_loop(0, heads, drain, 0)


def on_device(queries, key_vectors, value_vectors):
    n = lax.axis_size("seq")
    rows, width = queries.shape[1:]
    heads = width // DK
    values = value_vectors.shape[2]
    groups = -(-heads // 4)
    any_space = pl.BlockSpec(memory_space=pl.ANY)

    def body(*refs):
        kernel(n, heads, *refs)

    return pl.pallas_call(
        body,
        out_shape=jax.ShapeDtypeStruct((1, rows, values), BF16),
        in_specs=[any_space] * 3,
        out_specs=pl.BlockSpec(memory_space=pltpu.VMEM),
        scratch_shapes=[
            pltpu.VMEM((rows, width), BF16),
            pltpu.VMEM((LANES + rows, width), BF16),
            pltpu.VMEM((LANES + rows, values), BF16),
            pltpu.VMEM((heads, ROWS, rows), BF16),
            pltpu.VMEM((heads, ROWS, DV), F32),
            pltpu.VMEM((heads, ROWS, DV), BF16),
            pltpu.VMEM((heads, ROWS, DV), BF16),
            pltpu.VMEM((DK * (2 * heads - 1), 2 * LANES), BF16),
            pltpu.VMEM((groups, rows, LANES), BF16),
            pltpu.VMEM((heads, rows, LANES), BF16),
            pltpu.VMEM((heads, rows, 2 * DV), F32),
            pltpu.VMEM((heads, rows, DV), F32),
            pltpu.SemaphoreType.DMA((3,)),
            pltpu.SemaphoreType.DMA((2,)),
            pltpu.SemaphoreType.DMA((2,)),
            pltpu.SemaphoreType.DMA((heads,)),
            pltpu.SemaphoreType.DMA((heads,)),
        ],
        compiler_params=pltpu.CompilerParams(
            collective_id=0, has_side_effects=True, vmem_limit_bytes=48 * 2**20
        ),
    )(*[pltpu.with_memory_space_constraint(x, pltpu.HBM) for x in (queries, key_vectors, value_vectors)])


def solution(mesh):
    spec = P(("groups", "batch"), "seq", "head")
    return jax.shard_map(
        on_device, mesh=mesh, in_specs=(spec, spec, spec), out_specs=spec, check_vma=False
    )
```

time: 28.3 us -> 22.3 us (0.79)
  local copies, waits for them, and re-layouts: 4 us -> 0.97 us
  Pallas kernels: 24.1 us -> 21.2 us
    unnamed x7 -> x1, local copies, waits for them, and re-layouts: 4 us -> 0.97 us
    pallas_call x1, Pallas kernels: 24.1 us -> 21.2 us  [on_device(): pl.pallas_call(body, out_shape=jax.ShapeDtypeStruct((1, rows, values), BF...]
where the time goes in v2:
time: 22.3 us; the launch traced here: 22.1 us
  Pallas kernels  21.2 us (95%)
  local copies, waits for them, and re-layouts  0.97 us (4%)
    pallas_call x1, Pallas kernels, on_device(): pl.pallas_call(body, out_shape=jax.ShapeDtypeStruct((1, rows, values), BF...  21.2 us
    unnamed x1, local copies, waits for them, and re-layouts  0.97 us

profile of v2, /device:TPU:24, one launch (start us, length us, event | category | flops | bytes accessed | tf_op | source)
XLA Modules:
  0.0 22.1 jit_solution(14869803008957260819)
XLA Ops:
  0.0 21.2 %shard_map.37 = bf16[1,512,1024]{2,1,0:T(8,128)(2,1)S(1)} custom-call(bf16[1,512,128]{2,1,0:T(8,128)(2,1)} %refs_0_.1, bf16[1,512,128]{2,1,0:T(8,128)(2,1)} %refs_1_.1, bf16[1,512,1024]{2,1,0:T(8,128)(2,1)} %refs_2_.1), custom_call_target="tpu_custom_call" | custom-call | tf_op jit(solution)/shard_map/pallas_call | solution.py:325
  21.2 1.0 %copy.5 = bf16[1,512,1024]{2,1,0:T(8,128)(2,1)} copy(bf16[1,512,1024]{2,1,0:T(8,128)(2,1)S(1)} %shard_map.37) | data formatting | bytes 2097152

commit v3 on v2

--- a/solution.py
+++ b/solution.py
@@ -123,6 +123,9 @@
     @pl.when(has_next)
     def _():
         pl.semaphore_wait(barrier, 1)
+
+    @pl.when(has_prior & has_next)
+    def _():
         for copy in rim:
             copy.start()
 
@@ -183,6 +186,11 @@
                 sent[h] = own[h].astype(BF16)
                 chunk(h).start()
 
+    @pl.when(jnp.logical_not(has_prior) & has_next)
+    def _():
+        for copy in rim:
+            copy.start()
+
     picker[...] = pair_picker(heads)
     loads[2].wait()
     for group in range(groups):
@@ -192,112 +200,156 @@
         right = both[:, LANES:] + jnp.where((at == DK // 2) | (at >= DK), 1.0, 0.0)
         tails[group] = (left * right).astype(BF16)
 
-    @pl.when(has_prior)
-    def _():
-        for copy in rim:
-            copy.wait_recv()
-
-    def local(h, big):
-        lanes = pl.ds(pl.multiple_of(h * DV, DV), DV)
-        scale = jnp.where(iota((1, width), 1) >> 4 == h, 0.25, 0.0).astype(BF16)
-        row = iota((LANES, LANES), 0)
-        col = iota((LANES, LANES), 1)
+    row = iota((LANES, LANES), 0)
+    col = iota((LANES, LANES), 1)
+
+    def head_scale(h):
+        return jnp.where(iota((1, width), 1) >> 4 == h, 0.25, 0.0).astype(BF16)
+
+    def lanes_of(h):
+        return pl.ds(pl.multiple_of(h * DV, DV), DV)
+
+    def local(members, big):
         near = (col <= row) & (row - col < WINDOW)
         far = (col > row + half)[:half]
         start = big * BLOCK
         until = start + BLOCK
-        queries = q[start:until] * scale
-        scores = dot_nt(queries, kx[LANES:LANES + until])
-        raised = scores + 1.0
-        weights = raised * raised + 1.0
         causal = iota((BLOCK, BLOCK), 1) <= iota((BLOCK, BLOCK), 0)
-        diagonal = jnp.where(causal, weights[:, start:], 0.0)
-        if big:
-            weights = jnp.concatenate([weights[:, :start], diagonal], axis=1)
-        else:
-            weights = diagonal
-        sums[h, start:until] = dot(
-            weights.astype(BF16), with_ones(vx[LANES:LANES + until, lanes])
-        )
-        for small in range(BLOCK // LANES):
-            begin = start + small * LANES
-            part = scores[small * LANES:(small + 1) * LANES]
-            here = part[:, begin:begin + LANES]
+        scores = [
+            dot_nt(q[start:until] * head_scale(h), kx[LANES:LANES + until]) for h in members
+        ]
+        chains = []
+        for h, score in zip(members, scores):
+            for small in range(BLOCK // LANES):
+                begin = start + small * LANES
+                part = score[small * LANES:(small + 1) * LANES]
+                here = jnp.where(near, part[:, begin:begin + LANES], -jnp.inf)
+                low = jnp.max(here[half:], axis=1, keepdims=True)
+                if begin:
+                    before = jnp.where(far, part[:half, begin - LANES:begin], -jnp.inf)
+                    top = jnp.max(jnp.maximum(here[:half], before), axis=1, keepdims=True)
+                    chains.append((h, begin, here, before, top, low))
+                else:
+                    chains.append((h, begin, here, None, None, low))
+        for h, score in zip(members, scores):
+            raised = score + 1.0
+            weights = raised * raised + 1.0
+            diagonal = jnp.where(causal, weights[:, start:], 0.0)
+            if big:
+                weights = jnp.concatenate([weights[:, :start], diagonal], axis=1)
+            else:
+                weights = diagonal
+            sums[h, start:until] = dot(
+                weights.astype(BF16), with_ones(vx[LANES:LANES + until, lanes_of(h)])
+            )
+        shares = []
+        for h, begin, here, before, top, low in chains:
             if begin:
-                before = part[:half, begin - LANES:begin]
-                seen = far
+                share = jnp.concatenate(
+                    [
+                        jnp.concatenate(
+                            [jnp.exp(before - top), jnp.zeros((half, LANES), F32)], axis=0
+                        ),
+                        jnp.exp(here - jnp.concatenate([top, low], axis=0)),
+                    ],
+                    axis=1,
+                )
             else:
-                before = dot_nt(queries[:half], kx[0:LANES])
-                seen = far & has_prior
-            here = jnp.where(near, here, -jnp.inf)
-            before = jnp.where(seen, before, -jnp.inf)
-            top = jnp.max(jnp.maximum(here[:half], before), axis=1, keepdims=True)
-            low = jnp.max(here[half:], axis=1, keepdims=True)
-            shares = jnp.concatenate(
-                [
-                    jnp.concatenate(
-                        [jnp.exp(before - top), jnp.zeros((half, LANES), F32)], axis=0
-                    ),
-                    jnp.exp(here - jnp.concatenate([top, low], axis=0)),
-                ],
-                axis=1,
-            ).astype(BF16)
-            both = dot(shares, with_ones(vx[begin:begin + 2 * LANES, lanes]))
-            win[h, begin:begin + LANES] = both[:, :DV] * inverse(both[:, DV:])
-        pick = picker[pl.ds(pl.multiple_of(DK * (heads - 1 - h), DK), width)]
-        both = dot(q[start:until], pick)
-        phi_q[h, start:until] = (both[:, :LANES] * both[:, LANES:]).astype(BF16)
+                share = jnp.exp(here[half:] - low)
+            shares.append(share.astype(BF16))
+        windows = []
+        for (h, begin, *_), share in zip(chains, shares):
+            first = begin if begin else LANES
+            windows.append(
+                dot(share, with_ones(vx[first:begin + 2 * LANES, lanes_of(h)]))
+            )
+        for h in members:
+            pick = picker[pl.ds(pl.multiple_of(DK * (heads - 1 - h), DK), width)]
+            both = dot(q[start:until], pick)
+            phi_q[h, start:until] = (both[:, :LANES] * both[:, LANES:]).astype(BF16)
+        for (h, begin, *_), both in zip(chains, windows):
+            first = begin if begin else half
+            win[h, first:begin + LANES] = both[:, :DV] * inverse(both[:, DV:])
+
+    def edge():
+        queries = jnp.concatenate([q[0:half] * head_scale(h) for h in range(heads)], axis=0)
+        scores = dot_nt(queries, kx[0:2 * LANES])
+        at = iota((half, 2 * LANES), 1)
+        line = iota((half, 2 * LANES), 0)
+        seen = (at > line + half) & (at <= line + LANES) & ((at >= LANES) | has_prior)
+        shares = []
+        for h in range(heads):
+            score = jnp.where(seen, scores[h * half:(h + 1) * half], -jnp.inf)
+            peak = jnp.max(
+                jnp.maximum(score[:, :LANES], score[:, LANES:]), axis=1, keepdims=True
+            )
+            shares.append(jnp.exp(score - peak).astype(BF16))
+        for h in range(heads):
+            both = dot(shares[h], with_ones(vx[0:2 * LANES, h * DV:(h + 1) * DV]))
+            win[h, 0:half] = both[:, :DV] * inverse(both[:, DV:])
 
     def forward(h):
-        chunk(h).wait_recv()
-
-        @pl.when(has_next)
+        @pl.when(has_prior & (h >= 0) & (h < heads))
         def _():
-            sent[h] = (prior[h].astype(F32) + own[h]).astype(BF16)
-            chunk(h).start()
-
-    def finish(h):
-        lanes = pl.ds(pl.multiple_of(h * DV, DV), DV)
-        before = prior[h]
-        wide = before[DK * 8:DK * 9].astype(F32)
-        at = KEY_SUM_ROW - DK * 8
-        lane = iota((1, LANES), 1)
-        high = jnp.where(lane >> 5 == (h & 3), wide[at + 1:at + 2], 0.0)
-        key_sums = jnp.concatenate([wide[at:at + 1], high], axis=1).astype(BF16)
-        key_sums = jnp.broadcast_to(key_sums, (DV, 2 * LANES))
-        tail = jnp.concatenate([before[LANES:]] * (LANES // SLOT), axis=0)
-        slot = iota((LANES, 1), 0) >> 5
-        tail = jnp.where(slot == (h & 3), tail, jnp.zeros_like(tail))
-        state = jnp.concatenate([before[:LANES], tail], axis=0)
-        feats = jnp.concatenate([phi_q[h], tails[h >> 2]], axis=1)
-        total = sums[h, :, :DV] + dot(feats, state)
-        weight = sums[h, :, DV:] + dot_nt(feats, key_sums)
-        out_ref[0, :, lanes] = (win[h] + total * inverse(weight)).astype(BF16)
+            chunk(h).wait_recv()
+
+            @pl.when(has_next)
+            def _():
+                sent[h] = (prior[h].astype(F32) + own[h]).astype(BF16)
+                chunk(h).start()
+
+    def finish(members):
+        totals = []
+        for h in members:
+            before = prior[h]
+            wide = before[DK * 8:DK * 9].astype(F32)
+            at = KEY_SUM_ROW - DK * 8
+            lane = iota((1, LANES), 1)
+            high = jnp.where(lane >> 5 == (h & 3), wide[at + 1:at + 2], 0.0)
+            key_sums = jnp.concatenate([wide[at:at + 1], high], axis=1).astype(BF16)
+            key_sums = jnp.broadcast_to(key_sums, (DV, 2 * LANES))
+            tail = jnp.concatenate([before[LANES:]] * (LANES // SLOT), axis=0)
+            slot = iota((LANES, 1), 0) >> 5
+            tail = jnp.where(slot == (h & 3), tail, jnp.zeros_like(tail))
+            state = jnp.concatenate([before[:LANES], tail], axis=0)
+            feats = jnp.concatenate([phi_q[h], tails[h >> 2]], axis=1)
+            totals.append((dot(feats, state), dot_nt(feats, key_sums)))
+        for h, (total, weight) in zip(members, totals):
+            total = sums[h, :, :DV] + total
+            weight = sums[h, :, DV:] + weight
+            out_ref[0, :, lanes_of(h)] = (win[h] + total * inverse(weight)).astype(BF16)
 
     blocks = rows // BLOCK
-    late = jnp.minimum(jnp.maximum(place - 1, 0), heads // 2)
-    receive_lag = 4 * late + 1
-    finish_lag = 2 * late
-
-    def step(t, carry):
-        for big in range(blocks):
-            @pl.when(t < heads)
-            def _():
-                local(t, big)
-
-            arriving = blocks * t + big - receive_lag
-
-            @pl.when(has_prior & (arriving >= 0) & (arriving < heads))
-            def _():
-                forward(arriving)
-
-        @pl.when((t >= finish_lag) & (t < finish_lag + heads))
-        def _():
-            finish(t - finish_lag)
-
+    steps = heads // pair
+    units = blocks * steps
+    late = jnp.maximum(place - 1, 0)
+    lag = jnp.minimum(1 + 2 * late, units + 1)
+
+    def spread(t, carry):
+        members = [pair * t + e for e in range(pair)]
+        for order in range(blocks):
+            local(members, blocks - 1 - order)
+            forward(blocks * t + order - lag)
         return carry
 
-    lax.fori_loop(0, 2 * heads, step, 0)
+    lax.fori_loop(0, steps, spread, 0)
+    forward(units - lag)
+
+    @pl.when(has_prior)
+    def _():
+        for copy in rim:
+            copy.wait_recv()
+
+    edge()
+
+    def gather(t, carry):
+        members = [pair * t + e for e in range(pair)]
+        for h in members:
+            forward(units + 1 - lag + h)
+        finish(members)
+        return carry
+
+    lax.fori_loop(0, steps, gather, 0)
 
     @pl.when(has_next)
     def _():

time: 22.3 us -> 19 us (0.85)
  Pallas kernels: 21.2 us -> 17.9 us
    pallas_call x1, Pallas kernels: 21.2 us -> 17.9 us  [on_device(): pl.pallas_call(body, out_shape=jax.ShapeDtypeStruct((1, rows, values), BF...]
where the time goes in v3:
time: 19 us; the launch traced here: 18.9 us
  Pallas kernels  17.9 us (94%)
  local copies, waits for them, and re-layouts  0.97 us (5%)
    pallas_call x1, Pallas kernels, on_device(): pl.pallas_call(body, out_shape=jax.ShapeDtypeStruct((1, rows, values), BF...  17.9 us
    unnamed x1, local copies, waits for them, and re-layouts  0.97 us

profile of v3, /device:TPU:24, one launch (start us, length us, event | category | flops | bytes accessed | tf_op | source)
XLA Modules:
  0.0 18.9 jit_solution(2665032820117979400)
XLA Ops:
  0.0 17.9 %shard_map.37 = bf16[1,512,1024]{2,1,0:T(8,128)(2,1)S(1)} custom-call(bf16[1,512,128]{2,1,0:T(8,128)(2,1)} %refs_0_.1, bf16[1,512,128]{2,1,0:T(8,128)(2,1)} %refs_1_.1, bf16[1,512,1024]{2,1,0:T(8,128)(2,1)} %refs_2_.1), custom_call_target="tpu_custom_call" | custom-call | tf_op jit(solution)/shard_map/pallas_call | solution.py:377
  17.9 1.0 %copy.5 = bf16[1,512,1024]{2,1,0:T(8,128)(2,1)} copy(bf16[1,512,1024]{2,1,0:T(8,128)(2,1)S(1)} %shard_map.37) | data formatting | bytes 2097152

commit v4 on v3

--- a/solution.py
+++ b/solution.py
@@ -10,6 +10,7 @@
 WINDOW = 64
 ROWS = 160
 KEY_SUM_ROW = 137
+PIECES = 1
 LANES = 128
 BLOCK = 256
 SLOT = 32
@@ -73,7 +74,7 @@
 def kernel(
     n, heads,
     q_hbm, k_hbm, v_hbm, out_ref,
-    q, kx, vx, phi_k, own, sent, prior, picker, tails, phi_q, sums, win,
+    q, kx, vx, phi_k, own, sent, prior, picker, tails, phi_q, sums, win, rim_win,
     load_sem, rim_send, rim_recv, send_sem, recv_sem,
 ):
     rows = q.shape[0]
@@ -110,24 +111,16 @@
         for i, (src, dst) in enumerate(((k_hbm, kx), (v_hbm, vx)))
     ]
 
-    def chunk(h):
+    def chunk(h, piece):
+        lines = pl.ds(piece * (ROWS // PIECES), ROWS // PIECES)
         return pltpu.make_async_remote_copy(
-            src_ref=sent.at[h],
-            dst_ref=prior.at[h],
-            send_sem=send_sem.at[h],
-            recv_sem=recv_sem.at[h],
+            src_ref=sent.at[h, lines],
+            dst_ref=prior.at[h, lines],
+            send_sem=send_sem.at[h, piece],
+            recv_sem=recv_sem.at[h, piece],
             device_id={"seq": place + 1},
             device_id_type=MESH,
         )
-
-    @pl.when(has_next)
-    def _():
-        pl.semaphore_wait(barrier, 1)
-
-    @pl.when(has_prior & has_next)
-    def _():
-        for copy in rim:
-            copy.start()
 
     kx[0:half] = jnp.zeros((half, width), BF16)
     vx[0:half] = jnp.zeros((half, vx.shape[1]), BF16)
@@ -160,6 +153,15 @@
 
     def with_ones(values):
         return jnp.concatenate([values, jnp.ones((values.shape[0], DV), BF16)], axis=1)
+
+    @pl.when(has_next)
+    def _():
+        pl.semaphore_wait(barrier, 1)
+
+    @pl.when(has_prior & has_next)
+    def _():
+        for copy in rim:
+            copy.start()
 
     loads[1].wait()
 
@@ -184,12 +186,8 @@
         def _():
             for h in range(first, first + pair):
                 sent[h] = own[h].astype(BF16)
-                chunk(h).start()
-
-    @pl.when(jnp.logical_not(has_prior) & has_next)
-    def _():
-        for copy in rim:
-            copy.start()
+                for piece in range(PIECES):
+                    chunk(h, piece).start()
 
     picker[...] = pair_picker(heads)
     loads[2].wait()
@@ -286,17 +284,24 @@
             shares.append(jnp.exp(score - peak).astype(BF16))
         for h in range(heads):
             both = dot(shares[h], with_ones(vx[0:2 * LANES, h * DV:(h + 1) * DV]))
-            win[h, 0:half] = both[:, :DV] * inverse(both[:, DV:])
-
-    def forward(h):
-        @pl.when(has_prior & (h >= 0) & (h < heads))
+            rim_win[h] = both[:, :DV] * inverse(both[:, DV:])
+
+    def forward(first, end):
+        def one(h, carry):
+            for piece in range(PIECES):
+                chunk(h, piece).wait_recv()
+                lines = slice(piece * (ROWS // PIECES), (piece + 1) * (ROWS // PIECES))
+
+                @pl.when(has_next)
+                def _():
+                    sent[h, lines] = (prior[h, lines].astype(F32) + own[h, lines]).astype(BF16)
+                    chunk(h, piece).start()
+
+            return carry
+
+        @pl.when(has_prior)
         def _():
-            chunk(h).wait_recv()
-
-            @pl.when(has_next)
-            def _():
-                sent[h] = (prior[h].astype(F32) + own[h]).astype(BF16)
-                chunk(h).start()
+            lax.fori_loop(first, end, one, 0)
 
     def finish(members):
         totals = []
@@ -317,47 +322,73 @@
         for h, (total, weight) in zip(members, totals):
             total = sums[h, :, :DV] + total
             weight = sums[h, :, DV:] + weight
-            out_ref[0, :, lanes_of(h)] = (win[h] + total * inverse(weight)).astype(BF16)
+            linear = total * inverse(weight)
+            win[h, 0:half] = linear[0:half]
+            out_ref[0, half:rows, lanes_of(h)] = (win[h, half:rows] + linear[half:]).astype(BF16)
 
     blocks = rows // BLOCK
     steps = heads // pair
     units = blocks * steps
-    late = jnp.maximum(place - 1, 0)
-    lag = jnp.minimum(1 + 2 * late, units + 1)
+    delay = jnp.where(has_next, 10 + 10 * jnp.maximum(place - 1, 0), 1000)
+
+    def due(unit):
+        return jnp.minimum(jnp.maximum(5 * (unit + 1) - delay, 0) // 4, heads)
+
+    def needed(t):
+        return jnp.maximum(pair * t, due(units + t))
 
     def spread(t, carry):
         members = [pair * t + e for e in range(pair)]
         for order in range(blocks):
             local(members, blocks - 1 - order)
-            forward(blocks * t + order - lag)
+            unit = blocks * t + order
+            forward(due(unit - 1), due(unit))
         return carry
 
     lax.fori_loop(0, steps, spread, 0)
-    forward(units - lag)
-
-    @pl.when(has_prior)
+    forward(due(units - 1), due(units))
+
+    @pl.when(jnp.logical_not(has_prior) & has_next)
+    def _():
+        for copy in rim:
+            copy.start()
+
+    rim_late = place == 1
+
+    @pl.when(has_prior & jnp.logical_not(rim_late))
     def _():
         for copy in rim:
             copy.wait_recv()
 
-    edge()
+    @pl.when(jnp.logical_not(rim_late))
+    def _():
+        edge()
 
     def gather(t, carry):
         members = [pair * t + e for e in range(pair)]
-        for h in members:
-            forward(units + 1 - lag + h)
+        forward(needed(t), needed(t + 1))
         finish(members)
         return carry
 
     lax.fori_loop(0, steps, gather, 0)
 
+    @pl.when(rim_late)
+    def _():
+        for copy in rim:
+            copy.wait_recv()
+        edge()
+
+    for h in range(heads):
+        out_ref[0, 0:half, h * DV:(h + 1) * DV] = (rim_win[h] + win[h, 0:half]).astype(BF16)
+
     @pl.when(has_next)
     def _():
         for copy in rim:
             copy.wait_send()
 
         def drain(h, carry):
-            chunk(h).wait_send()
+            for piece in range(PIECES):
+                chunk(h, piece).wait_send()
             return carry
 
         lax.fori_loop(0, heads, drain, 0)
@@ -392,11 +423,12 @@
             pltpu.VMEM((heads, rows, LANES), BF16),
             pltpu.VMEM((heads, rows, 2 * DV), F32),
             pltpu.VMEM((heads, rows, DV), F32),
+            pltpu.VMEM((heads, WINDOW, DV), F32),
             pltpu.SemaphoreType.DMA((3,)),
             pltpu.SemaphoreType.DMA((2,)),
             pltpu.SemaphoreType.DMA((2,)),
-            pltpu.SemaphoreType.DMA((heads,)),
-            pltpu.SemaphoreType.DMA((heads,)),
+            pltpu.SemaphoreType.DMA((heads, PIECES)),
+            pltpu.SemaphoreType.DMA((heads, PIECES)),
         ],
         compiler_params=pltpu.CompilerParams(
             collective_id=0, has_side_effects=True, vmem_limit_bytes=48 * 2**20

time: 19 us -> 18 us (0.947)
  Pallas kernels: 17.9 us -> 16.8 us
    pallas_call x1, Pallas kernels: 17.9 us -> 16.8 us  [on_device(): pl.pallas_call(body, out_shape=jax.ShapeDtypeStruct((1, rows, values), BF...]
where the time goes in v4:
time: 18 us; the launch traced here: 17.8 us
  Pallas kernels  16.8 us (93%)
  local copies, waits for them, and re-layouts  0.97 us (5%)
    pallas_call x1, Pallas kernels, on_device(): pl.pallas_call(body, out_shape=jax.ShapeDtypeStruct((1, rows, values), BF...  16.8 us
    unnamed x1, local copies, waits for them, and re-layouts  0.97 us

profile of v4, /device:TPU:24, one launch (start us, length us, event | category | flops | bytes accessed | tf_op | source)
XLA Modules:
  0.0 17.8 jit_solution(17728876512370054182)
XLA Ops:
  0.0 16.8 %shard_map.37 = bf16[1,512,1024]{2,1,0:T(8,128)(2,1)S(1)} custom-call(bf16[1,512,128]{2,1,0:T(8,128)(2,1)} %refs_0_.1, bf16[1,512,128]{2,1,0:T(8,128)(2,1)} %refs_1_.1, bf16[1,512,1024]{2,1,0:T(8,128)(2,1)} %refs_2_.1), custom_call_target="tpu_custom_call" | custom-call | tf_op jit(solution)/shard_map/pallas_call | solution.py:408
  16.8 1.0 %copy.5 = bf16[1,512,1024]{2,1,0:T(8,128)(2,1)} copy(bf16[1,512,1024]{2,1,0:T(8,128)(2,1)S(1)} %shard_map.37) | data formatting | bytes 2097152

commit v5 on v4

--- a/solution.py
+++ b/solution.py
@@ -332,7 +332,7 @@
     delay = jnp.where(has_next, 10 + 10 * jnp.maximum(place - 1, 0), 1000)
 
     def due(unit):
-        return jnp.minimum(jnp.maximum(5 * (unit + 1) - delay, 0) // 4, heads)
+        return jnp.minimum(jnp.maximum(6 * (unit + 1) - delay, 0) // 4, heads)
 
     def needed(t):
         return jnp.maximum(pair * t, due(units + t))

time: 18 us -> 17.7 us (0.983)
  Pallas kernels: 16.8 us -> 16.6 us
    pallas_call x1, Pallas kernels: 16.8 us -> 16.6 us  [on_device(): pl.pallas_call(body, out_shape=jax.ShapeDtypeStruct((1, rows, values), BF...]
where the time goes in v5:
time: 17.7 us; the launch traced here: 17.6 us
  Pallas kernels  16.6 us (94%)
  local copies, waits for them, and re-layouts  0.97 us (5%)
    pallas_call x1, Pallas kernels, on_device(): pl.pallas_call(body, out_shape=jax.ShapeDtypeStruct((1, rows, values), BF...  16.6 us
    unnamed x1, local copies, waits for them, and re-layouts  0.97 us

profile of v5, /device:TPU:24, one launch (start us, length us, event | category | flops | bytes accessed | tf_op | source)
XLA Modules:
  0.0 17.6 jit_solution(5015781402088527838)
XLA Ops:
  0.0 16.6 %shard_map.37 = bf16[1,512,1024]{2,1,0:T(8,128)(2,1)S(1)} custom-call(bf16[1,512,128]{2,1,0:T(8,128)(2,1)} %refs_0_.1, bf16[1,512,128]{2,1,0:T(8,128)(2,1)} %refs_1_.1, bf16[1,512,1024]{2,1,0:T(8,128)(2,1)} %refs_2_.1), custom_call_target="tpu_custom_call" | custom-call | tf_op jit(solution)/shard_map/pallas_call | solution.py:408
  16.6 1.0 %copy.5 = bf16[1,512,1024]{2,1,0:T(8,128)(2,1)} copy(bf16[1,512,1024]{2,1,0:T(8,128)(2,1)S(1)} %shard_map.37) | data formatting | bytes 2097152
